TPU v7x, 32 devices: a whole 2x2x4 slice. The times are simulated.
32 devices in a mesh: req: 16 (over z, y, x), tp: 2 (over core).
Axes of the slice: x: 2, y: 2, z: 4, core: 2. Of those that a mesh axis runs over, the one named last changes fastest.
Arguments:
- hidden_in: bfloat16 [256, 2048], P('req'), may hold values from -6 to 6
- query: bfloat16 [256, 2048], P('req', 'tp'), may hold values from -200 to 200
- new_kv: bfloat16 [256, 4096], P('req', 'tp'), may hold values from -6 to 6
- pool_cache: bfloat16 [1280, 32, 4096], P('req', None, 'tp'), may hold values from -7 to 7
- prompt_table: int32 [32, 24], P('req'), may hold values from 0 to 79, as said below
- prompt_len: int32 [32], P('req'), may hold values from 32 to 768
- req_group: int32 [256], P('req'), may hold values from 0 to 1, as said below
- cont_table: int32 [256, 2], P('req'), may hold values from 0 to 79, as said below
- cont_len: int32 [256], P('req'), may hold values from 1 to 63
- migration: int32 [96, 2], P('req'), may hold values from 0 to 15, as said below
- diff_lambda: float32 [8], P('tp'), may hold values from 0.2 to 0.8
- out_weight: bfloat16 [2048, 2048], P('tp'), may hold values from -0.125 to 0.125
- norm_gain: float32 [2048], replicated, may hold values from 0.1 to 1.9
Outputs:
- hidden_out: bfloat16 [256, 2048], P('req')
- normed_out: bfloat16 [256, 2048], P('req')
- arrived: bfloat16 [128, 64, 4096], P('req', None, 'tp')
Inputs may be any that keep to these rules, and one draw needn't show every extreme that they name: `prompt_table`: entries are pages local to the row's index of req; with cont_table, each of a device's 80 pages appears exactly once. `cont_table`: local pages, each page of a device once together with prompt_table. `req_group`: A group index local to the device; every group of a device has a request. `migration`: each device lists 6 rows: a distinct local request slot and a destination offset 1 to 4 along req (with wrap); at most 2 rows of a device share an offset, and that many is reached.
All inputs are finite; a program needn't handle non-finite values.
Results may differ from a plain program's by a relative error of at most 0.012.
Values may be sent and summed in bfloat16 or wider, within the bound.
No kernel may reach another device: no remote copies, remote signals or barrier semaphores. Data moves between devices by JAX's collectives and lax.ppermute only.
A program may use at most 128 MiB of HBM per device.

v0:
```python
import functools

import jax
import jax.numpy as jnp
from jax import lax
from jax.experimental import pallas as pl
from jax.experimental.pallas import tpu as pltpu
from jax.sharding import PartitionSpec as P

MIG_REACH = 4
MIG_CAP = 2
KEY = 128
ROWS = 16

SMEM = pl.BlockSpec(memory_space=pltpu.SMEM)
VMEM = pl.BlockSpec(memory_space=pltpu.VMEM)
HBM = pl.BlockSpec(memory_space=pltpu.HBM)
VMEM_BYTES = 40 * 1024 * 1024
SMALL_VMEM_BYTES = 8 * 1024 * 1024


def pinned(*arrays):
    return [pltpu.with_memory_space_constraint(array, pltpu.HBM) for array in arrays]


def shifted(value, axis, steps):
    count = lax.axis_size(axis)
    pairs = [(source, (source + steps) % count) for source in range(count)]
    return lax.ppermute(value, axis, pairs)


def send_kernel(offsets, table_in, length_in, migration_in, new_in, pool, *refs):
    outs = refs[:MIG_REACH]
    table, length, migration, holder, new_held, new_rows, sems, small_sems = refs[MIG_REACH:]
    small = [
        pltpu.make_async_copy(source, target, small_sems.at[n])
        for n, (source, target) in enumerate(
            zip((table_in, length_in, migration_in, new_in), (table, length, migration, new_held))
        )
    ]
    for copy in small:
        copy.start()
    for copy in small[:3]:
        copy.wait()
    entries = migration.shape[1]
    pages, page = table.shape[0], pool.shape[1]
    for place in range(MIG_REACH * MIG_CAP):
        holder[place] = -1
    odd = lax.rem(lax.axis_index("req"), 2)
    where = []
    for n, (on_even, on_odd) in enumerate(offsets):
        offset = on_even + odd * (on_odd - on_even)
        for i in range(MIG_CAP):
            where.append((n * MIG_CAP + i, (offset - 1) * MIG_CAP + i, outs[n].at[i]))
    for e in range(entries):
        rank = jnp.int32(0)
        for before in range(e):
            rank += (migration[1, before] == migration[1, e]).astype(jnp.int32)
        holder[(migration[1, e] - 1) * MIG_CAP + rank] = migration[0, e]

    def page_copy(n, place, out, j):
        slot = jnp.maximum(holder[place], 0)
        return pltpu.make_async_copy(pool.at[table[j, slot]], out.at[pl.ds(j * page, page)], sems.at[n, j])

    def used(place, j):
        slot = holder[place]
        return (slot >= 0) & (length[jnp.maximum(slot, 0)] >= j * page)

    for n, place, out in where:
        for j in range(pages):

            @pl.when(used(place, j))
            def _():
                page_copy(n, place, out, j).start()

    small[3].wait()
    new_rows[...] = new_held[...].astype(jnp.float32)
    for n, place, out in where:
        slot = holder[place]
        safe = jnp.maximum(slot, 0)
        last = jnp.where(slot >= 0, length[safe], -1)
        for j in range(pages):

            @pl.when(used(place, j))
            def _():
                page_copy(n, place, out, j).wait()

            for low in range(j * page, (j + 1) * page, ROWS):

                @pl.when(last < low)
                def _():
                    out[pl.ds(low, ROWS)] = jnp.zeros((ROWS, out.shape[1]), out.dtype)

                @pl.when((last >= low) & (last < low + ROWS))
                def _():
                    held = out[pl.ds(low, ROWS)].astype(jnp.float32)
                    pos = low + lax.broadcasted_iota(jnp.int32, held.shape, 0)
                    new = jnp.where(pos == last, new_rows[pl.ds(safe, 1)], 0.0)
                    out[pl.ds(low, ROWS)] = jnp.where(pos < last, held, new).astype(out.dtype)


def send_slots(offsets, cont_table, cont_len, migration, new_kv, pool):
    span = cont_table.shape[0] * pool.shape[1]
    width = pool.shape[2]
    return pl.pallas_call(
        functools.partial(send_kernel, offsets),
        out_shape=[jax.ShapeDtypeStruct((MIG_CAP, span, width), pool.dtype)] * MIG_REACH,
        in_specs=[HBM] * 5,
        out_specs=[VMEM] * MIG_REACH,
        scratch_shapes=[
            pltpu.SMEM(cont_table.shape, jnp.int32),
            pltpu.SMEM(cont_len.shape, jnp.int32),
            pltpu.SMEM(migration.shape, jnp.int32),
            pltpu.SMEM((MIG_REACH * MIG_CAP,), jnp.int32),
            pltpu.VMEM(new_kv.shape, new_kv.dtype),
            pltpu.VMEM(new_kv.shape, jnp.float32),
            pltpu.SemaphoreType.DMA((MIG_REACH * MIG_CAP, cont_table.shape[0])),
            pltpu.SemaphoreType.DMA((4,)),
        ],
        compiler_params=pltpu.CompilerParams(vmem_limit_bytes=VMEM_BYTES),
        name="send_slots",
    )(*pinned(cont_table, cont_len, migration, new_kv, pool))


def column(values, count):
    rows = lax.broadcasted_iota(jnp.int32, (count, 1), 0)
    out = jnp.zeros((count, 1), jnp.int32)
    for r in range(count):
        out = jnp.where(rows == r, values[r], out)
    return out


def attention_kernel(low, prompt_table, prompt_len, req_group, cont_table, cont_len, lam, query, new_ref, *refs):
    prior = refs[:-6]
    weight, pool, out, held, weight_held, sems = refs[-6:]
    groups, prompt_pages = prompt_table.shape
    cont_pages, reqs = cont_table.shape
    page = pool.shape[1]
    span = prompt_pages * page
    own = cont_pages * page
    start = groups * span
    head_width = pool.shape[2] // lam.shape[0]
    value_width = head_width - 2 * KEY
    width = held.shape[1]
    heads = width // head_width
    columns = pl.ds(low * head_width, width)

    for g in range(groups):

        @pl.loop(0, prompt_pages)
        def _(j):
            at = pl.multiple_of(g * span + j * page, page)
            pltpu.make_async_copy(pool.at[prompt_table[g, j], :, columns], held.at[pl.ds(at, page)], sems.at[0]).start()

    @pl.loop(0, reqs)
    def _(r):
        for j in range(cont_pages):
            at = pl.multiple_of(start + r * own + j * page, page)
            pltpu.make_async_copy(pool.at[cont_table[j, r], :, columns], held.at[pl.ds(at, page)], sems.at[0]).start()

    rows = pl.ds(low * value_width, weight_held.shape[0])
    weight_copy = pltpu.make_async_copy(weight.at[rows], weight_held, sems.at[1])
    weight_copy.start()

    group_of = column(req_group, reqs)
    length_of = column(cont_len, reqs)
    biases = []
    pos = lax.broadcasted_iota(jnp.int32, (reqs, span), 1)
    for g in range(groups):
        live = (group_of == g) & (pos < prompt_len[g])
        biases.append(jnp.where(live, 0.0, -1e30))
    key = lax.broadcasted_iota(jnp.int32, (reqs, reqs * own), 1)
    pos = key - own * lax.broadcasted_iota(jnp.int32, (reqs, reqs * own), 0)
    biases.append(jnp.where((pos >= 0) & (pos < length_of), 0.0, -1e30))
    live = jnp.concatenate(biases, axis=1) == 0.0

    pltpu.make_async_copy(held, held, sems.at[0]).wait()

    scale = KEY**-0.5
    mixed = []
    for h in range(heads):
        first = h * head_width
        weights, new_weights = [], []
        for i in range(2):
            q = query[:, pl.ds((2 * (low + h) + i) * KEY, KEY)]
            cols = pl.ds(first + i * KEY, KEY)
            new_cols = pl.ds(low * head_width + first + i * KEY, KEY)
            score = lax.dot_general(
                q, held[:, cols], (((1,), (1,)), ((), ())), preferred_element_type=jnp.float32
            )
            score = jnp.where(live, score * scale, -1e30)
            new = jnp.sum(q.astype(jnp.float32) * new_ref[:, new_cols].astype(jnp.float32), axis=1, keepdims=True) * scale
            top = jnp.maximum(jnp.max(score, axis=1, keepdims=True), new)
            score = jnp.exp(score - top)
            new = jnp.exp(new - top)
            inverse = 1.0 / (jnp.sum(score, axis=1, keepdims=True) + new)
            weights.append((score * inverse).astype(jnp.bfloat16))
            new_weights.append((new * inverse).astype(jnp.bfloat16).astype(jnp.float32))
        cols = pl.ds(first + 2 * KEY, value_width)
        mixture = jnp.dot(jnp.concatenate(weights, axis=0), held[:, cols], preferred_element_type=jnp.float32)
        new_value = new_ref[:, pl.ds(low * head_width + first + 2 * KEY, value_width)].astype(jnp.float32)
        one = mixture[:reqs] + new_weights[0] * new_value
        two = mixture[reqs:] + new_weights[1] * new_value
        diff = one - lam[low + h] * two
        norm = lax.rsqrt(jnp.mean(diff * diff, axis=1, keepdims=True) + 1e-05)
        mixed.append((diff * norm * 0.8).astype(jnp.bfloat16))
    weight_copy.wait()
    mixed = jnp.concatenate(mixed, axis=1)
    product = jnp.dot(mixed, weight_held[...], preferred_element_type=jnp.float32)
    for part in prior:
        product = product + part[...]
    out[...] = product.astype(out.dtype)


def attention(query, new_kv, pool, prompt_table, prompt_len, req_group, cont_table, cont_len, lam, weight, low, high, prior):
    reqs = query.shape[0]
    page = pool.shape[1]
    heads = lam.shape[0]
    keys = (prompt_table.size + cont_table.size) * page
    width = pool.shape[2] // heads * (high - low)
    rows = weight.shape[0] // heads * (high - low)
    return pl.pallas_call(
        functools.partial(attention_kernel, low),
        out_shape=jax.ShapeDtypeStruct((reqs, weight.shape[1]), jnp.bfloat16 if high == heads else jnp.float32),
        in_specs=[SMEM] * 6 + [VMEM] * (2 + len(prior)) + [HBM, HBM],
        out_specs=VMEM,
        scratch_shapes=[
            pltpu.VMEM((keys, width), pool.dtype),
            pltpu.VMEM((rows, weight.shape[1]), weight.dtype),
            pltpu.SemaphoreType.DMA((2,)),
        ],
        compiler_params=pltpu.CompilerParams(vmem_limit_bytes=VMEM_BYTES),
        cost_estimate=pl.CostEstimate(
            flops=4 * reqs * keys * width + 2 * reqs * rows * weight.shape[1],
            bytes_accessed=2 * (keys * width + rows * weight.shape[1]),
            transcendentals=reqs * keys * 2 * (high - low),
        ),
        name="attention",
    )(prompt_table, prompt_len, req_group, cont_table, cont_len, lam, query, new_kv, *prior, *pinned(weight, pool))


def finish_kernel(count, hidden, gain, *refs):
    parts = refs[:count]
    hidden_out, normed_out = refs[count:]
    total = parts[0][...].astype(jnp.float32)
    for part in parts[1:]:
        total = total + part[...].astype(jnp.float32)
    summed = hidden[...].astype(jnp.float32) + total
    norm = lax.rsqrt(jnp.mean(summed * summed, axis=1, keepdims=True) + 1e-05)
    hidden_out[...] = summed.astype(hidden_out.dtype)
    normed_out[...] = (summed * norm * gain[...]).astype(normed_out.dtype)


def finish(hidden, gain, parts):
    shape = jax.ShapeDtypeStruct(hidden.shape, jnp.bfloat16)
    return pl.pallas_call(
        functools.partial(finish_kernel, len(parts)),
        out_shape=[shape, shape],
        in_specs=[VMEM] * (2 + len(parts)),
        out_specs=[VMEM, VMEM],
        compiler_params=pltpu.CompilerParams(vmem_limit_bytes=SMALL_VMEM_BYTES),
        name="finish",
    )(hidden, gain.reshape(1, -1), *parts)


def gather_kernel(choose, *refs):
    parts, out, sems = refs[:-2], refs[-2], refs[-1]
    for n, (place, options) in enumerate(choose()):
        target = out.at[pl.ds(place, MIG_CAP)]
        for part, taken in options:
            copy = pltpu.make_async_copy(parts[part], target, sems.at[n])
            if taken is None:
                copy.start()
            else:
                pl.when(taken)(copy.start)
    for n in range(MIG_REACH):
        pltpu.make_async_copy(parts[0], out.at[pl.ds(n * MIG_CAP, MIG_CAP)], sems.at[n]).wait()


def arrive(parts, choose):
    slots = MIG_REACH * MIG_CAP
    return pl.pallas_call(
        functools.partial(gather_kernel, choose),
        out_shape=jax.ShapeDtypeStruct((slots,) + parts[0].shape[1:], parts[0].dtype),
        in_specs=[VMEM] * len(parts),
        out_specs=HBM,
        scratch_shapes=[pltpu.SemaphoreType.DMA((MIG_REACH,))],
        compiler_params=pltpu.CompilerParams(vmem_limit_bytes=SMALL_VMEM_BYTES),
        name="arrive",
    )(*parts)


def routed(value, targets):
    count, width = lax.axis_size("req"), lax.axis_size("tp")
    pairs = []
    for s in range(count):
        for t in range(width):
            target = targets(s, t % 2)
            if target is not None:
                target = target % count
                pairs.append((s * width + t, target * width + (t ^ 1 if target == s else t)))
    return lax.ppermute(value, ("req", "tp"), pairs)


def turn(s, steps):
    return s - s % MIG_REACH + (s + steps) % MIG_REACH


def route_early(s, odd):
    if s % 2 == 0:
        return s + 1
    return turn(s, 3) if odd else s + 3


def route_late(s, odd):
    return s + 3 if s % 2 == 0 else s + 1


def lift_two(s, odd):
    return s + MIG_REACH if s % MIG_REACH < 2 else s


def lift_early(s, odd):
    return s + MIG_REACH if odd and s % 2 == 0 else None


def choose_straight():
    return [(n * MIG_CAP, [(n, None)]) for n in range(MIG_REACH)]


def choose_relayed():
    col = lax.rem(lax.axis_index("req"), MIG_REACH)
    odd_core = lax.rem(lax.axis_index("tp"), 2) == 1
    odd = lax.rem(col, 2) == 1
    even = jnp.logical_not(odd)
    return [
        (0, [(2, odd), (4, even)]),
        (2, [(0, col >= 2), (1, col < 2)]),
        (4, [(4, odd), (2, even & jnp.logical_not(odd_core)), (3, even & odd_core)]),
        (6, [(5, None)]),
    ]


def can_relay():
    count = lax.axis_size("req")
    return MIG_REACH == 4 and count % MIG_REACH == 0 and count > MIG_REACH and lax.axis_size("tp") % 2 == 0


def shards(
    hidden_in,
    query,
    new_kv,
    pool_cache,
    prompt_table,
    prompt_len,
    req_group,
    cont_table,
    cont_len,
    migration,
    diff_lambda,
    out_weight,
    norm_gain,
):
    cont_table, migration = cont_table.T, migration.T
    heads = diff_lambda.shape[0]
    half = heads // 2
    attend = functools.partial(
        attention, query, new_kv, pool_cache, prompt_table, prompt_len, req_group, cont_table, cont_len, diff_lambda, out_weight
    )
    send = (cont_table, cont_len, migration, new_kv, pool_cache)
    prior = [attend(0, half, [])] if half else []
    if can_relay():
        two, four, early, late = send_slots(((2, 2), (4, 4), (1, 3), (3, 1)), *send)
        two = routed(two, lambda s, odd: turn(s, 2))
        four = shifted(four, "req", 4)
        early = routed(early, route_early)
        prior, two = lax.optimization_barrier((prior, two))
        two_up = routed(two, lift_two)
        two, late = lax.optimization_barrier((two, late))
        late = routed(late, route_late)
        early_up = routed(early, lift_early)
        received, choose = (two, two_up, early, early_up, late, four), choose_relayed
    else:
        outgoing = send_slots(tuple((o, o) for o in range(1, MIG_REACH + 1)), *send)
        received = [shifted(part, "req", o + 1) for o, part in enumerate(outgoing)]
        choose = choose_straight
    partial = attend(half, heads, prior)
    if lax.axis_size("tp") == 2:
        parts = [partial, shifted(partial, "tp", 1)]
    else:
        parts = [lax.psum(partial, "tp")]
    hidden_out, normed_out = finish(hidden_in, norm_gain, parts)
    arrived = arrive(received, choose)
    return (hidden_out, normed_out, arrived)


def solution(mesh):
    placed = (
        P("req", None),
        P("req", "tp"),
        P("req", "tp"),
        P("req", None, "tp"),
        P("req", None),
        P("req"),
        P("req"),
        P("req", None),
        P("req"),
        P("req", None),
        P("tp"),
        P("tp", None),
        P(),
    )
    return jax.shard_map(
        shards,
        mesh=mesh,
        in_specs=placed,
        out_specs=(P("req", None), P("req", None), P("req", None, "tp")),
        check_vma=False,
    )
```

profile of v0, /device:TPU:1, one launch (start us, length us, event | category | flops | bytes accessed | tf_op | source)
XLA Modules:
  0.0 40.5 jit_solution(13000135417984636334)
XLA Ops:
  0.6 0.0 copy-start
  0.6 0.0 copy-start.1
  0.7 0.0 copy-start.3
  0.7 0.0 copy-start.5
  0.7 0.0 copy-start.6
  0.7 0.0 copy-start.7
  0.7 0.0 copy-start.8
  0.7 0.0 copy-start.9
  0.7 2.7 %send_slots.1 = (bf16[2,64,2048]{2,1,0:T(8,128)(2,1)S(1)}, bf16[2,64,2048]{2,1,0:T(8,128)(2,1)S(1)}, bf16[2,64,2048]{2,1,0:T(8,128)(2,1)S(1)}, bf16[2,64,2048]{2,1,0:T(8,128)(2,1)S(1)}) custom-call(s32[2,16]{1,0:T(2,128)} %bitcast.3, s32[16]{0:T(128)} %cont_len.3, s32[2,6]{1,0:T(2,128)} %bitcast.7, bf16[16,2048]{1,0:T(8,128)(2,1)} %new_ref.3, ...), custom_call_target="tpu_custom_call" | custom-call | tf_op jit(solution)/shard_map/send_slots/pallas_call | solution.py:105
  3.4 2.1 %collective-permute-start = (bf16[2,64,2048]{2,1,0:T(8,128)(2,1)S(1)}, bf16[2,64,2048]{2,1,0:T(8,128)(2,1)S(1)}, u32[]{:S(2)}, u32[]{:S(2)}) collective-permute-start(bf16[2,64,2048]{2,1,0:T(8,128)(2,1)S(1)} %get-tuple-element.13), channel_id=1, source_target_pairs={{0,4},{1,5},{2,6},{3,7},{4,0},{5,1},{6,2},{7,3},{8,12},{9,13},{10,... | collective-permute-start | bytes 1572872 | tf_op jit(solution)/shard_map/ppermute | solution.py:302
  5.5 1.2 %collective-permute-start.3 = (bf16[2,64,2048]{2,1,0:T(8,128)(2,1)S(1)}, bf16[2,64,2048]{2,1,0:T(8,128)(2,1)S(1)}, u32[]{:S(2)}, u32[]{:S(2)}) collective-permute-start(bf16[2,64,2048]{2,1,0:T(8,128)(2,1)S(1)} %get-tuple-element.20), channel_id=1, source_target_pairs={{0,2},{1,3},{2,8},{3,1},{4,6},{5,7},{6,12},{7,5},{8,10},{9,11},{10... | collective-permute-start | bytes 1572872 | tf_op jit(solution)/shard_map/ppermute | solution.py:302
  6.7 1.2 %collective-permute-start.6 = (bf16[2,64,2048]{2,1,0:T(8,128)(2,1)S(1)}, bf16[2,64,2048]{2,1,0:T(8,128)(2,1)S(1)}, u32[]{:S(2)}, u32[]{:S(2)}) collective-permute-start(bf16[2,64,2048]{2,1,0:T(8,128)(2,1)S(1)} %get-tuple-element.22), channel_id=1, source_target_pairs={{0,8},{2,10},{4,12},{6,14},{8,16},{10,18},{12,20},{14,22},{16,24},... | collective-permute-start | bytes 1572872 | tf_op jit(solution)/shard_map/ppermute | solution.py:29
  7.9 0.0 copy-done
  7.9 0.0 copy-done.1
  7.9 0.0 copy-done.3
  7.9 0.0 copy-done.5
  8.0 5.7 %attention.2.refs_0_ = f32[16,2048]{1,0:T(8,128)S(1)} custom-call(s32[2,24]{1,0:T(2,128)S(1)} %copy-done.6, s32[2]{0:T(128)S(1)} %copy-done.7, s32[16]{0:T(128)S(1)} %copy-done.8, s32[2,16]{1,0:T(2,128)S(1)} %bitcast.4, s32[16]{0:T(128)S(1)} %copy-done.5, f32[4]{0:T(128)S(1)} %copy-done.9, bf16[16,1024]{1,0:T(8,128)(2,1)S(1)} %copy-done.1, ...), custom_call_target="tpu_custom_call" | custom-call | flops 201326592 | bytes 7340032 | tf_op jit(solution)/shard_map/attention/pallas_call | solution.py:222
  13.7 3.4 %collective-permute-done.refs_0_ = bf16[2,64,2048]{2,1,0:T(8,128)(2,1)S(1)} collective-permute-done((bf16[2,64,2048]{2,1,0:T(8,128)(2,1)S(1)}, bf16[2,64,2048]{2,1,0:T(8,128)(2,1)S(1)}, u32[]{:S(2)}, u32[]{:S(2)}) %collective-permute-start) | collective-permute-done | bytes 524320 | tf_op jit(solution)/shard_map/ppermute | solution.py:302
  17.1 1.2 %collective-permute-start.2 = (bf16[2,64,2048]{2,1,0:T(8,128)(2,1)S(1)}, bf16[2,64,2048]{2,1,0:T(8,128)(2,1)S(1)}, u32[]{:S(2)}, u32[]{:S(2)}) collective-permute-start(bf16[2,64,2048]{2,1,0:T(8,128)(2,1)S(1)} %collective-permute-done.refs_0_), channel_id=1, source_target_pairs={{0,8},{1,9},{2,10},{3,11},{4,5},{5,4},{6,7},{7,6},{8,16},{9,17},{1... | collective-permute-start | bytes 1572872 | tf_op jit(solution)/shard_map/ppermute | solution.py:302
  18.4 2.4 %collective-permute-start.5 = (bf16[2,64,2048]{2,1,0:T(8,128)(2,1)S(1)}, bf16[2,64,2048]{2,1,0:T(8,128)(2,1)S(1)}, u32[]{:S(2)}, u32[]{:S(2)}) collective-permute-start(bf16[2,64,2048]{2,1,0:T(8,128)(2,1)S(1)} %get-tuple-element.21), channel_id=1, source_target_pairs={{0,6},{1,7},{2,4},{3,5},{4,10},{5,11},{6,8},{7,9},{8,14},{9,15},{1... | collective-permute-start | bytes 1572872 | tf_op jit(solution)/shard_map/ppermute | solution.py:302
  20.7 0.0 collective-permute-done.3.refs_2_
  20.7 3.1 %collective-permute-start.4 = (bf16[2,64,2048]{2,1,0:T(8,128)(2,1)S(1)}, bf16[2,64,2048]{2,1,0:T(8,128)(2,1)S(1)}, u32[]{:S(2)}, u32[]{:S(2)}) collective-permute-start(bf16[2,64,2048]{2,1,0:T(8,128)(2,1)S(1)} %collective-permute-done.3.refs_2_), channel_id=1, source_target_pairs={{1,9},{5,13},{9,17},{13,21},{17,25},{21,29},{25,1},{29,5}} | collective-permute-start | bytes 1572872 | tf_op jit(solution)/shard_map/ppermute | solution.py:302
  23.9 5.7 %attention.3.refs_0_ = bf16[16,2048]{1,0:T(8,128)(2,1)S(1)} custom-call(s32[2,24]{1,0:T(2,128)S(1)} %copy-done.6, s32[2]{0:T(128)S(1)} %copy-done.7, s32[16]{0:T(128)S(1)} %copy-done.8, s32[2,16]{1,0:T(2,128)S(1)} %bitcast.5, s32[16]{0:T(128)S(1)} %copy-done.5, f32[4]{0:T(128)S(1)} %copy-done.9, bf16[16,1024]{1,0:T(8,128)(2,1)S(1)} %copy-done.1, ...), custom_call_target="tpu_custom_call" | custom-call | flops 201326592 | bytes 7340032 | tf_op jit(solution)/shard_map/attention/pallas_call | solution.py:222
  29.6 0.1 collective-permute-start.1
  29.7 1.2 %collective-permute-done.1.refs_1_ = bf16[16,2048]{1,0:T(8,128)(2,1)S(1)} collective-permute-done((bf16[16,2048]{1,0:T(8,128)(2,1)S(1)}, bf16[16,2048]{1,0:T(8,128)(2,1)S(1)}, u32[]{:S(2)}, u32[]{:S(2)}) %collective-permute-start.1) | collective-permute-done | bytes 65568 | tf_op jit(solution)/shard_map/ppermute | solution.py:29
  30.9 0.0 copy-done.2
  30.9 0.8 %finish.1 = (bf16[16,2048]{1,0:T(8,128)(2,1)}, bf16[16,2048]{1,0:T(8,128)(2,1)}) custom-call(bf16[16,2048]{1,0:T(8,128)(2,1)S(1)} %copy-done.2, f32[1,2048]{1,0:T(1,128)S(1)} %bitcast.6, bf16[16,2048]{1,0:T(8,128)(2,1)S(1)} %attention.3.refs_0_, bf16[16,2048]{1,0:T(8,128)(2,1)S(1)} %collective-permute-done.1.refs_1_), custom_call_target="tpu_custom_call" | custom-call | tf_op jit(solution)/shard_map/finish/pallas_call | solution.py:256
  31.7 0.0 collective-permute-done.6.refs_5_
  31.7 4.6 %collective-permute-done.5.refs_4_ = bf16[2,64,2048]{2,1,0:T(8,128)(2,1)S(1)} collective-permute-done((bf16[2,64,2048]{2,1,0:T(8,128)(2,1)S(1)}, bf16[2,64,2048]{2,1,0:T(8,128)(2,1)S(1)}, u32[]{:S(2)}, u32[]{:S(2)}) %collective-permute-start.5) | collective-permute-done | bytes 524320 | tf_op jit(solution)/shard_map/ppermute | solution.py:302
  36.3 0.0 collective-permute-done.2.refs_1_
  36.3 2.9 %collective-permute-done.4.refs_3_ = bf16[2,64,2048]{2,1,0:T(8,128)(2,1)S(1)} collective-permute-done((bf16[2,64,2048]{2,1,0:T(8,128)(2,1)S(1)}, bf16[2,64,2048]{2,1,0:T(8,128)(2,1)S(1)}, u32[]{:S(2)}, u32[]{:S(2)}) %collective-permute-start.4) | collective-permute-done | bytes 524320 | tf_op jit(solution)/shard_map/ppermute | solution.py:302
  39.2 1.3 %arrive.1 = bf16[8,64,2048]{2,1,0:T(8,128)(2,1)} custom-call(bf16[2,64,2048]{2,1,0:T(8,128)(2,1)S(1)} %collective-permute-done.refs_0_, bf16[2,64,2048]{2,1,0:T(8,128)(2,1)S(1)} %collective-permute-done.2.refs_1_, bf16[2,64,2048]{2,1,0:T(8,128)(2,1)S(1)} %collective-permute-done.3.refs_2_, bf16[2,64,2048]{2,1,0:T(8,128)(2,1)S(1)} %collective-permute-done.4.refs_3_, ...), custom_call_target="tpu_custom_call" | custom-call | tf_op jit(solution)/shard_map/arrive/pallas_call | solution.py:282
  (7 shorter events, 0.0 us)
Async XLA Ops:
  0.6 7.3 %copy-start = (bf16[16,2048]{1,0:T(8,128)(2,1)S(1)}, bf16[16,2048]{1,0:T(8,128)(2,1)}, u32[]{:S(2)}) copy-start(bf16[16,2048]{1,0:T(8,128)(2,1)} %new_ref.3) | copy-start | bytes 196612
  0.6 7.3 %copy-start.1 = (bf16[16,1024]{1,0:T(8,128)(2,1)S(1)}, bf16[16,1024]{1,0:T(8,128)(2,1)}, u32[]{:S(2)}) copy-start(bf16[16,1024]{1,0:T(8,128)(2,1)} %query.3) | copy-start | bytes 98308
  0.7 7.3 %copy-start.3 = (s32[16,2]{0,1:T(2,128)S(1)}, s32[16,2]{0,1:T(2,128)}, u32[]{:S(2)}) copy-start(s32[16,2]{0,1:T(2,128)} %param.20) | copy-start | bytes 388
  0.7 7.3 %copy-start.5 = (s32[16]{0:T(128)S(1)}, s32[16]{0:T(128)}, u32[]{:S(2)}) copy-start(s32[16]{0:T(128)} %cont_len.3) | copy-start | bytes 196
  0.7 7.2 %copy-start.6 = (s32[2,24]{1,0:T(2,128)S(1)}, s32[2,24]{1,0:T(2,128)}, u32[]{:S(2)}) copy-start(s32[2,24]{1,0:T(2,128)} %prompt_table.3) | copy-start | bytes 580
  0.7 7.2 %copy-start.7 = (s32[2]{0:T(128)S(1)}, s32[2]{0:T(128)}, u32[]{:S(2)}) copy-start(s32[2]{0:T(128)} %prompt_len.3) | copy-start | bytes 28
  0.7 7.2 %copy-start.8 = (s32[16]{0:T(128)S(1)}, s32[16]{0:T(128)}, u32[]{:S(2)}) copy-start(s32[16]{0:T(128)} %req_group.3) | copy-start | bytes 196
  0.7 7.2 %copy-start.9 = (f32[4]{0:T(128)S(1)}, f32[4]{0:T(128)}, u32[]{:S(2)}) copy-start(f32[4]{0:T(128)} %lam.3) | copy-start | bytes 52
  3.4 13.7 %collective-permute-start = (bf16[2,64,2048]{2,1,0:T(8,128)(2,1)S(1)}, bf16[2,64,2048]{2,1,0:T(8,128)(2,1)S(1)}, u32[]{:S(2)}, u32[]{:S(2)}) collective-permute-start(bf16[2,64,2048]{2,1,0:T(8,128)(2,1)S(1)} %get-tuple-element.13), channel_id=1, source_target_pairs={{0,4},{1,5},{2,6},{3,7},{4,0},{5,1},{6,2},{7,3},{8,12},{9,13},{10,... | collective-permute-start | bytes 1572872 | tf_op jit(solution)/shard_map/ppermute | solution.py:302
  5.5 15.3 %collective-permute-start.3 = (bf16[2,64,2048]{2,1,0:T(8,128)(2,1)S(1)}, bf16[2,64,2048]{2,1,0:T(8,128)(2,1)S(1)}, u32[]{:S(2)}, u32[]{:S(2)}) collective-permute-start(bf16[2,64,2048]{2,1,0:T(8,128)(2,1)S(1)} %get-tuple-element.20), channel_id=1, source_target_pairs={{0,2},{1,3},{2,8},{3,1},{4,6},{5,7},{6,12},{7,5},{8,10},{9,11},{10... | collective-permute-start | bytes 1572872 | tf_op jit(solution)/shard_map/ppermute | solution.py:302
  6.7 25.0 %collective-permute-start.6 = (bf16[2,64,2048]{2,1,0:T(8,128)(2,1)S(1)}, bf16[2,64,2048]{2,1,0:T(8,128)(2,1)S(1)}, u32[]{:S(2)}, u32[]{:S(2)}) collective-permute-start(bf16[2,64,2048]{2,1,0:T(8,128)(2,1)S(1)} %get-tuple-element.22), channel_id=1, source_target_pairs={{0,8},{2,10},{4,12},{6,14},{8,16},{10,18},{12,20},{14,22},{16,24},... | collective-permute-start | bytes 1572872 | tf_op jit(solution)/shard_map/ppermute | solution.py:29
  17.1 19.2 %collective-permute-start.2 = (bf16[2,64,2048]{2,1,0:T(8,128)(2,1)S(1)}, bf16[2,64,2048]{2,1,0:T(8,128)(2,1)S(1)}, u32[]{:S(2)}, u32[]{:S(2)}) collective-permute-start(bf16[2,64,2048]{2,1,0:T(8,128)(2,1)S(1)} %collective-permute-done.refs_0_), channel_id=1, source_target_pairs={{0,8},{1,9},{2,10},{3,11},{4,5},{5,4},{6,7},{7,6},{8,16},{9,17},{1... | collective-permute-start | bytes 1572872 | tf_op jit(solution)/shard_map/ppermute | solution.py:302
  18.4 12.6 %copy-start.2 = (bf16[16,2048]{1,0:T(8,128)(2,1)S(1)}, bf16[16,2048]{1,0:T(8,128)(2,1)}, u32[]{:S(2)}) copy-start(bf16[16,2048]{1,0:T(8,128)(2,1)} %hidden.1) | copy-start | bytes 196612
  18.4 12.6 %copy-start.4 = (f32[2048]{0:T(1024)S(1)}, f32[2048]{0:T(1024)}, u32[]{:S(2)}) copy-start(f32[2048]{0:T(1024)} %param.25) | copy-start | bytes 24580
  18.4 17.9 %collective-permute-start.5 = (bf16[2,64,2048]{2,1,0:T(8,128)(2,1)S(1)}, bf16[2,64,2048]{2,1,0:T(8,128)(2,1)S(1)}, u32[]{:S(2)}, u32[]{:S(2)}) collective-permute-start(bf16[2,64,2048]{2,1,0:T(8,128)(2,1)S(1)} %get-tuple-element.21), channel_id=1, source_target_pairs={{0,6},{1,7},{2,4},{3,5},{4,10},{5,11},{6,8},{7,9},{8,14},{9,15},{1... | collective-permute-start | bytes 1572872 | tf_op jit(solution)/shard_map/ppermute | solution.py:302
  20.7 18.4 %collective-permute-start.4 = (bf16[2,64,2048]{2,1,0:T(8,128)(2,1)S(1)}, bf16[2,64,2048]{2,1,0:T(8,128)(2,1)S(1)}, u32[]{:S(2)}, u32[]{:S(2)}) collective-permute-start(bf16[2,64,2048]{2,1,0:T(8,128)(2,1)S(1)} %collective-permute-done.3.refs_2_), channel_id=1, source_target_pairs={{1,9},{5,13},{9,17},{13,21},{17,25},{21,29},{25,1},{29,5}} | collective-permute-start | bytes 1572872 | tf_op jit(solution)/shard_map/ppermute | solution.py:302
  29.6 1.3 %collective-permute-start.1 = (bf16[16,2048]{1,0:T(8,128)(2,1)S(1)}, bf16[16,2048]{1,0:T(8,128)(2,1)S(1)}, u32[]{:S(2)}, u32[]{:S(2)}) collective-permute-start(bf16[16,2048]{1,0:T(8,128)(2,1)S(1)} %attention.3.refs_0_), channel_id=1, source_target_pairs={{0,1},{1,0},{2,3},{3,2},{4,5},{5,4},{6,7},{7,6},{8,9},{9,8},{10,11... | collective-permute-start | bytes 196616 | tf_op jit(solution)/shard_map/ppermute | solution.py:29
where the time goes:
time: 41.1 us; the launch traced here: 40.5 us
  Pallas kernels  16.2 us (39%)
  waiting for transfers between devices  12.2 us (30%)
  starting transfers between devices  11.3 us (27%)
  between operations  0.78 us (2%)
    pallas_call x2, Pallas kernels, attention(): pl.pallas_call(functools.partial(attention_kernel, low), out_shape=jax.Sh...  11.4 us
    ppermute x5, waiting for transfers between devices, routed(): return lax.ppermute(value, ('req', 'tp'), pairs)  10.9 us
    ppermute x5, starting transfers between devices, routed(): return lax.ppermute(value, ('req', 'tp'), pairs)  10.1 us
    pallas_call x1, Pallas kernels, send_slots(): pl.pallas_call(functools.partial(send_kernel, offsets), out_shape=[jax.Sh...  2.65 us
    pallas_call x1, Pallas kernels, arrive(): pl.pallas_call(functools.partial(gather_kernel, choose), out_shape=jax.Sh...  1.34 us
    ppermute x2, starting transfers between devices, shifted(): return lax.ppermute(value, axis, pairs)  1.3 us
    ppermute x2, waiting for transfers between devices, shifted(): return lax.ppermute(value, axis, pairs)  1.24 us
  transfers between devices with their start and end apart: 7, of which 4 were waited for; matrix products, arithmetic and copies ran while one was open for 0% of the time, Pallas kernels for 30%

commit v1 on v0

--- a/solution.py
+++ b/solution.py
@@ -263,31 +263,31 @@
     )(hidden, gain.reshape(1, -1), *parts)
 
 
-def gather_kernel(choose, *refs):
-    parts, out, sems = refs[:-2], refs[-2], refs[-1]
-    for n, (place, options) in enumerate(choose()):
-        target = out.at[pl.ds(place, MIG_CAP)]
-        for part, taken in options:
-            copy = pltpu.make_async_copy(parts[part], target, sems.at[n])
-            if taken is None:
-                copy.start()
-            else:
-                pl.when(taken)(copy.start)
-    for n in range(MIG_REACH):
-        pltpu.make_async_copy(parts[0], out.at[pl.ds(n * MIG_CAP, MIG_CAP)], sems.at[n]).wait()
-
-
-def arrive(parts, choose):
+def gather_kernel(choose, count, *refs):
+    parts, out, sems = refs[:count], refs[-2], refs[-1]
+    copies = [
+        (pltpu.make_async_copy(parts[part], out.at[pl.ds(place, MIG_CAP)], sems.at[n]), taken)
+        for n, (place, part, taken) in enumerate(choose())
+    ]
+    for copy, taken in copies:
+        pl.when(taken)(copy.start)
+    for copy, taken in copies:
+        pl.when(taken)(copy.wait)
+
+
+def arrive(parts, choose, rest=None):
     slots = MIG_REACH * MIG_CAP
+    extra = [] if rest is None else pinned(rest)
     return pl.pallas_call(
-        functools.partial(gather_kernel, choose),
+        functools.partial(gather_kernel, choose, len(parts)),
         out_shape=jax.ShapeDtypeStruct((slots,) + parts[0].shape[1:], parts[0].dtype),
-        in_specs=[VMEM] * len(parts),
+        in_specs=[VMEM] * len(parts) + [HBM] * len(extra),
         out_specs=HBM,
-        scratch_shapes=[pltpu.SemaphoreType.DMA((MIG_REACH,))],
+        scratch_shapes=[pltpu.SemaphoreType.DMA((2 * MIG_REACH,))],
+        input_output_aliases={len(parts): 0} if extra else {},
         compiler_params=pltpu.CompilerParams(vmem_limit_bytes=SMALL_VMEM_BYTES),
         name="arrive",
-    )(*parts)
+    )(*parts, *extra)
 
 
 def routed(value, targets):
@@ -325,20 +325,31 @@
 
 
 def choose_straight():
-    return [(n * MIG_CAP, [(n, None)]) for n in range(MIG_REACH)]
-
-
-def choose_relayed():
+    return [(n * MIG_CAP, n, True) for n in range(MIG_REACH)]
+
+
+def where_am_i():
     col = lax.rem(lax.axis_index("req"), MIG_REACH)
+    odd = lax.rem(col, 2) == 1
     odd_core = lax.rem(lax.axis_index("tp"), 2) == 1
-    odd = lax.rem(col, 2) == 1
-    even = jnp.logical_not(odd)
+    return col, odd, jnp.logical_not(odd), odd_core
+
+
+def choose_sooner():
+    col, odd, even, odd_core = where_am_i()
     return [
-        (0, [(2, odd), (4, even)]),
-        (2, [(0, col >= 2), (1, col < 2)]),
-        (4, [(4, odd), (2, even & jnp.logical_not(odd_core)), (3, even & odd_core)]),
-        (6, [(5, None)]),
+        (0, 1, odd),
+        (0, 2, even),
+        (2, 0, col >= 2),
+        (4, 2, odd),
+        (4, 1, even & jnp.logical_not(odd_core)),
+        (6, 3, True),
     ]
+
+
+def choose_later():
+    col, odd, even, odd_core = where_am_i()
+    return [(2, 0, col < 2), (4, 1, even & odd_core)]
 
 
 def can_relay():
@@ -374,23 +385,22 @@
         two = routed(two, lambda s, odd: turn(s, 2))
         four = shifted(four, "req", 4)
         early = routed(early, route_early)
-        prior, two = lax.optimization_barrier((prior, two))
+        prior, two, late = lax.optimization_barrier((prior, two, late))
         two_up = routed(two, lift_two)
-        two, late = lax.optimization_barrier((two, late))
         late = routed(late, route_late)
         early_up = routed(early, lift_early)
-        received, choose = (two, two_up, early, early_up, late, four), choose_relayed
     else:
         outgoing = send_slots(tuple((o, o) for o in range(1, MIG_REACH + 1)), *send)
-        received = [shifted(part, "req", o + 1) for o, part in enumerate(outgoing)]
-        choose = choose_straight
+        arrived = arrive([shifted(part, "req", o + 1) for o, part in enumerate(outgoing)], choose_straight)
     partial = attend(half, heads, prior)
     if lax.axis_size("tp") == 2:
         parts = [partial, shifted(partial, "tp", 1)]
     else:
         parts = [lax.psum(partial, "tp")]
     hidden_out, normed_out = finish(hidden_in, norm_gain, parts)
-    arrived = arrive(received, choose)
+    if can_relay():
+        sooner = arrive((two, early, late, four), choose_sooner)
+        arrived = arrive((two_up, early_up), choose_later, sooner)
     return (hidden_out, normed_out, arrived)
 
 

time: 41.1 us -> 41.8 us (1.017)
  Pallas kernels: 16.2 us -> 16.9 us
    pallas_call x1 -> x2, Pallas kernels: 1.34 us -> 2.07 us  [arrive(): pl.pallas_call(functools.partial(gather_kernel, choose, len(parts)), out_...]
  transfers between devices with their start and end apart: 7 -> 7, of which waited for: 4 -> 4; matrix products, arithmetic and copies ran while one was open for 0% -> 0% of each run, Pallas kernels for 30% -> 32%
where the time goes in v1:
time: 41.8 us; the launch traced here: 41.4 us
  Pallas kernels  16.9 us (40%)
  waiting for transfers between devices  12.4 us (30%)
  starting transfers between devices  11.3 us (27%)
  between operations  0.8 us (2%)
    pallas_call x2, Pallas kernels, attention(): pl.pallas_call(functools.partial(attention_kernel, low), out_shape=jax.Sh...  11.4 us
    ppermute x5, waiting for transfers between devices, routed(): return lax.ppermute(value, ('req', 'tp'), pairs)  11.1 us
    ppermute x5, starting transfers between devices, routed(): return lax.ppermute(value, ('req', 'tp'), pairs)  9.82 us
    pallas_call x1, Pallas kernels, send_slots(): pl.pallas_call(functools.partial(send_kernel, offsets), out_shape=[jax.Sh...  2.62 us
    pallas_call x2, Pallas kernels, arrive(): pl.pallas_call(functools.partial(gather_kernel, choose, len(parts)), out_...  2.07 us
    ppermute x2, starting transfers between devices, shifted(): return lax.ppermute(value, axis, pairs)  1.45 us
    ppermute x2, waiting for transfers between devices, shifted(): return lax.ppermute(value, axis, pairs)  1.24 us
  transfers between devices with their start and end apart: 7, of which 4 were waited for; matrix products, arithmetic and copies ran while one was open for 0% of the time, Pallas kernels for 32%

profile of v1, /device:TPU:1, one launch (start us, length us, event | category | flops | bytes accessed | tf_op | source)
XLA Modules:
  0.0 41.4 jit_solution(18157656320397301640)
XLA Ops:
  0.6 0.0 copy-start
  0.6 0.0 copy-start.1
  0.7 0.0 copy-start.3
  0.7 0.0 copy-start.5
  0.7 0.0 copy-start.6
  0.7 0.0 copy-start.7
  0.7 0.0 copy-start.8
  0.7 0.0 copy-start.9
  0.7 2.6 %send_slots.1 = (bf16[2,64,2048]{2,1,0:T(8,128)(2,1)S(1)}, bf16[2,64,2048]{2,1,0:T(8,128)(2,1)S(1)}, bf16[2,64,2048]{2,1,0:T(8,128)(2,1)S(1)}, bf16[2,64,2048]{2,1,0:T(8,128)(2,1)S(1)}) custom-call(s32[2,16]{1,0:T(2,128)} %bitcast.3, s32[16]{0:T(128)} %cont_len.3, s32[2,6]{1,0:T(2,128)} %bitcast.7, bf16[16,2048]{1,0:T(8,128)(2,1)} %new_ref.3, ...), custom_call_target="tpu_custom_call" | custom-call | tf_op jit(solution)/shard_map/send_slots/pallas_call | solution.py:105
  3.3 2.1 %collective-permute-start = (bf16[2,64,2048]{2,1,0:T(8,128)(2,1)S(1)}, bf16[2,64,2048]{2,1,0:T(8,128)(2,1)S(1)}, u32[]{:S(2)}, u32[]{:S(2)}) collective-permute-start(bf16[2,64,2048]{2,1,0:T(8,128)(2,1)S(1)} %get-tuple-element.12), channel_id=1, source_target_pairs={{0,4},{1,5},{2,6},{3,7},{4,0},{5,1},{6,2},{7,3},{8,12},{9,13},{10,... | collective-permute-start | bytes 1572872 | tf_op jit(solution)/shard_map/ppermute | solution.py:302
  5.4 1.2 %collective-permute-start.3 = (bf16[2,64,2048]{2,1,0:T(8,128)(2,1)S(1)}, bf16[2,64,2048]{2,1,0:T(8,128)(2,1)S(1)}, u32[]{:S(2)}, u32[]{:S(2)}) collective-permute-start(bf16[2,64,2048]{2,1,0:T(8,128)(2,1)S(1)} %get-tuple-element.18), channel_id=1, source_target_pairs={{0,2},{1,3},{2,8},{3,1},{4,6},{5,7},{6,12},{7,5},{8,10},{9,11},{10... | collective-permute-start | bytes 1572872 | tf_op jit(solution)/shard_map/ppermute | solution.py:302
  6.6 1.4 %collective-permute-start.6 = (bf16[2,64,2048]{2,1,0:T(8,128)(2,1)S(1)}, bf16[2,64,2048]{2,1,0:T(8,128)(2,1)S(1)}, u32[]{:S(2)}, u32[]{:S(2)}) collective-permute-start(bf16[2,64,2048]{2,1,0:T(8,128)(2,1)S(1)} %get-tuple-element.20), channel_id=1, source_target_pairs={{0,8},{2,10},{4,12},{6,14},{8,16},{10,18},{12,20},{14,22},{16,24},... | collective-permute-start | bytes 1572872 | tf_op jit(solution)/shard_map/ppermute | solution.py:29
  8.0 0.0 copy-done.5
  8.0 0.0 copy-done.6
  8.0 0.0 copy-done.7
  8.0 0.0 copy-done.8
  8.0 5.7 %attention.2.refs_0_ = f32[16,2048]{1,0:T(8,128)S(1)} custom-call(s32[2,24]{1,0:T(2,128)S(1)} %copy-done.6, s32[2]{0:T(128)S(1)} %copy-done.7, s32[16]{0:T(128)S(1)} %copy-done.8, s32[2,16]{1,0:T(2,128)S(1)} %bitcast.4, s32[16]{0:T(128)S(1)} %copy-done.5, f32[4]{0:T(128)S(1)} %copy-done.9, bf16[16,1024]{1,0:T(8,128)(2,1)S(1)} %copy-done.1, ...), custom_call_target="tpu_custom_call" | custom-call | flops 201326592 | bytes 7340032 | tf_op jit(solution)/shard_map/attention/pallas_call | solution.py:222
  13.7 3.3 %collective-permute-done.refs_0_ = bf16[2,64,2048]{2,1,0:T(8,128)(2,1)S(1)} collective-permute-done((bf16[2,64,2048]{2,1,0:T(8,128)(2,1)S(1)}, bf16[2,64,2048]{2,1,0:T(8,128)(2,1)S(1)}, u32[]{:S(2)}, u32[]{:S(2)}) %collective-permute-start) | collective-permute-done | bytes 524320 | tf_op jit(solution)/shard_map/ppermute | solution.py:302
  17.1 2.0 %collective-permute-start.5 = (bf16[2,64,2048]{2,1,0:T(8,128)(2,1)S(1)}, bf16[2,64,2048]{2,1,0:T(8,128)(2,1)S(1)}, u32[]{:S(2)}, u32[]{:S(2)}) collective-permute-start(bf16[2,64,2048]{2,1,0:T(8,128)(2,1)S(1)} %get-tuple-element.19), channel_id=1, source_target_pairs={{0,6},{1,7},{2,4},{3,5},{4,10},{5,11},{6,8},{7,9},{8,14},{9,15},{1... | collective-permute-start | bytes 1572872 | tf_op jit(solution)/shard_map/ppermute | solution.py:302
  19.1 1.4 %collective-permute-start.2 = (bf16[2,64,2048]{2,1,0:T(8,128)(2,1)S(1)}, bf16[2,64,2048]{2,1,0:T(8,128)(2,1)S(1)}, u32[]{:S(2)}, u32[]{:S(2)}) collective-permute-start(bf16[2,64,2048]{2,1,0:T(8,128)(2,1)S(1)} %collective-permute-done.refs_0_), channel_id=1, source_target_pairs={{0,8},{1,9},{2,10},{3,11},{4,5},{5,4},{6,7},{7,6},{8,16},{9,17},{1... | collective-permute-start | bytes 1572872 | tf_op jit(solution)/shard_map/ppermute | solution.py:302
  20.5 0.0 collective-permute-done.3.refs_1_
  20.5 3.2 %collective-permute-start.4 = (bf16[2,64,2048]{2,1,0:T(8,128)(2,1)S(1)}, bf16[2,64,2048]{2,1,0:T(8,128)(2,1)S(1)}, u32[]{:S(2)}, u32[]{:S(2)}) collective-permute-start(bf16[2,64,2048]{2,1,0:T(8,128)(2,1)S(1)} %collective-permute-done.3.refs_1_), channel_id=1, source_target_pairs={{1,9},{5,13},{9,17},{13,21},{17,25},{21,29},{25,1},{29,5}} | collective-permute-start | bytes 1572872 | tf_op jit(solution)/shard_map/ppermute | solution.py:302
  23.7 5.7 %attention.3.refs_0_ = bf16[16,2048]{1,0:T(8,128)(2,1)S(1)} custom-call(s32[2,24]{1,0:T(2,128)S(1)} %copy-done.6, s32[2]{0:T(128)S(1)} %copy-done.7, s32[16]{0:T(128)S(1)} %copy-done.8, s32[2,16]{1,0:T(2,128)S(1)} %bitcast.5, s32[16]{0:T(128)S(1)} %copy-done.5, f32[4]{0:T(128)S(1)} %copy-done.9, bf16[16,1024]{1,0:T(8,128)(2,1)S(1)} %copy-done.1, ...), custom_call_target="tpu_custom_call" | custom-call | flops 201326592 | bytes 7340032 | tf_op jit(solution)/shard_map/attention/pallas_call | solution.py:222
  29.4 0.1 collective-permute-start.1
  29.5 1.2 %collective-permute-done.1.refs_1_ = bf16[16,2048]{1,0:T(8,128)(2,1)S(1)} collective-permute-done((bf16[16,2048]{1,0:T(8,128)(2,1)S(1)}, bf16[16,2048]{1,0:T(8,128)(2,1)S(1)}, u32[]{:S(2)}, u32[]{:S(2)}) %collective-permute-start.1) | collective-permute-done | bytes 65568 | tf_op jit(solution)/shard_map/ppermute | solution.py:29
  30.7 0.8 %finish.1 = (bf16[16,2048]{1,0:T(8,128)(2,1)}, bf16[16,2048]{1,0:T(8,128)(2,1)}) custom-call(bf16[16,2048]{1,0:T(8,128)(2,1)S(1)} %copy-done.2, f32[1,2048]{1,0:T(1,128)S(1)} %bitcast.6, bf16[16,2048]{1,0:T(8,128)(2,1)S(1)} %attention.3.refs_0_, bf16[16,2048]{1,0:T(8,128)(2,1)S(1)} %collective-permute-done.1.refs_1_), custom_call_target="tpu_custom_call" | custom-call | tf_op jit(solution)/shard_map/finish/pallas_call | solution.py:256
  31.5 0.0 collective-permute-done.6.refs_3_
  31.5 3.3 %collective-permute-done.5.refs_2_ = bf16[2,64,2048]{2,1,0:T(8,128)(2,1)S(1)} collective-permute-done((bf16[2,64,2048]{2,1,0:T(8,128)(2,1)S(1)}, bf16[2,64,2048]{2,1,0:T(8,128)(2,1)S(1)}, u32[]{:S(2)}, u32[]{:S(2)}) %collective-permute-start.5) | collective-permute-done | bytes 524320 | tf_op jit(solution)/shard_map/ppermute | solution.py:302
  34.8 1.0 %arrive.2.refs_2_ = bf16[8,64,2048]{2,1,0:T(8,128)(2,1)} custom-call(bf16[2,64,2048]{2,1,0:T(8,128)(2,1)S(1)} %collective-permute-done.refs_0_, bf16[2,64,2048]{2,1,0:T(8,128)(2,1)S(1)} %collective-permute-done.3.refs_1_, bf16[2,64,2048]{2,1,0:T(8,128)(2,1)S(1)} %collective-permute-done.5.refs_2_, bf16[2,64,2048]{2,1,0:T(8,128)(2,1)S(1)} %collective-permute-done.6.refs_3_), custom_call_target="tpu_custom_call" | custom-call | tf_op jit(solution)/shard_map/arrive/pallas_call | solution.py:281
  35.8 0.0 collective-permute-done.2.refs_0_
  35.8 4.5 %collective-permute-done.4.refs_1_ = bf16[2,64,2048]{2,1,0:T(8,128)(2,1)S(1)} collective-permute-done((bf16[2,64,2048]{2,1,0:T(8,128)(2,1)S(1)}, bf16[2,64,2048]{2,1,0:T(8,128)(2,1)S(1)}, u32[]{:S(2)}, u32[]{:S(2)}) %collective-permute-start.4) | collective-permute-done | bytes 524320 | tf_op jit(solution)/shard_map/ppermute | solution.py:302
  40.3 1.0 %arrive.3 = bf16[8,64,2048]{2,1,0:T(8,128)(2,1)} custom-call(bf16[2,64,2048]{2,1,0:T(8,128)(2,1)S(1)} %collective-permute-done.2.refs_0_, bf16[2,64,2048]{2,1,0:T(8,128)(2,1)S(1)} %collective-permute-done.4.refs_1_, bf16[8,64,2048]{2,1,0:T(8,128)(2,1)} %arrive.2.refs_2_), custom_call_target="tpu_custom_call", output_to_operand_aliasing={{}: (2, {})} | custom-call | tf_op jit(solution)/shard_map/arrive/pallas_call | solution.py:281
  (8 shorter events, 0.0 us)
Async XLA Ops:
  0.6 7.3 %copy-start = (bf16[16,2048]{1,0:T(8,128)(2,1)S(1)}, bf16[16,2048]{1,0:T(8,128)(2,1)}, u32[]{:S(2)}) copy-start(bf16[16,2048]{1,0:T(8,128)(2,1)} %new_ref.3) | copy-start | bytes 196612
  0.6 7.3 %copy-start.1 = (bf16[16,1024]{1,0:T(8,128)(2,1)S(1)}, bf16[16,1024]{1,0:T(8,128)(2,1)}, u32[]{:S(2)}) copy-start(bf16[16,1024]{1,0:T(8,128)(2,1)} %query.3) | copy-start | bytes 98308
  0.7 7.3 %copy-start.3 = (s32[16,2]{0,1:T(2,128)S(1)}, s32[16,2]{0,1:T(2,128)}, u32[]{:S(2)}) copy-start(s32[16,2]{0,1:T(2,128)} %param.20) | copy-start | bytes 388
  0.7 7.3 %copy-start.5 = (s32[16]{0:T(128)S(1)}, s32[16]{0:T(128)}, u32[]{:S(2)}) copy-start(s32[16]{0:T(128)} %cont_len.3) | copy-start | bytes 196
  0.7 7.3 %copy-start.6 = (s32[2,24]{1,0:T(2,128)S(1)}, s32[2,24]{1,0:T(2,128)}, u32[]{:S(2)}) copy-start(s32[2,24]{1,0:T(2,128)} %prompt_table.3) | copy-start | bytes 580
  0.7 7.3 %copy-start.7 = (s32[2]{0:T(128)S(1)}, s32[2]{0:T(128)}, u32[]{:S(2)}) copy-start(s32[2]{0:T(128)} %prompt_len.3) | copy-start | bytes 28
  0.7 7.3 %copy-start.8 = (s32[16]{0:T(128)S(1)}, s32[16]{0:T(128)}, u32[]{:S(2)}) copy-start(s32[16]{0:T(128)} %req_group.3) | copy-start | bytes 196
  0.7 7.3 %copy-start.9 = (f32[4]{0:T(128)S(1)}, f32[4]{0:T(128)}, u32[]{:S(2)}) copy-start(f32[4]{0:T(128)} %lam.3) | copy-start | bytes 52
  3.3 13.7 %collective-permute-start = (bf16[2,64,2048]{2,1,0:T(8,128)(2,1)S(1)}, bf16[2,64,2048]{2,1,0:T(8,128)(2,1)S(1)}, u32[]{:S(2)}, u32[]{:S(2)}) collective-permute-start(bf16[2,64,2048]{2,1,0:T(8,128)(2,1)S(1)} %get-tuple-element.12), channel_id=1, source_target_pairs={{0,4},{1,5},{2,6},{3,7},{4,0},{5,1},{6,2},{7,3},{8,12},{9,13},{10,... | collective-permute-start | bytes 1572872 | tf_op jit(solution)/shard_map/ppermute | solution.py:302
  5.4 15.1 %collective-permute-start.3 = (bf16[2,64,2048]{2,1,0:T(8,128)(2,1)S(1)}, bf16[2,64,2048]{2,1,0:T(8,128)(2,1)S(1)}, u32[]{:S(2)}, u32[]{:S(2)}) collective-permute-start(bf16[2,64,2048]{2,1,0:T(8,128)(2,1)S(1)} %get-tuple-element.18), channel_id=1, source_target_pairs={{0,2},{1,3},{2,8},{3,1},{4,6},{5,7},{6,12},{7,5},{8,10},{9,11},{10... | collective-permute-start | bytes 1572872 | tf_op jit(solution)/shard_map/ppermute | solution.py:302
  6.6 24.9 %collective-permute-start.6 = (bf16[2,64,2048]{2,1,0:T(8,128)(2,1)S(1)}, bf16[2,64,2048]{2,1,0:T(8,128)(2,1)S(1)}, u32[]{:S(2)}, u32[]{:S(2)}) collective-permute-start(bf16[2,64,2048]{2,1,0:T(8,128)(2,1)S(1)} %get-tuple-element.20), channel_id=1, source_target_pairs={{0,8},{2,10},{4,12},{6,14},{8,16},{10,18},{12,20},{14,22},{16,24},... | collective-permute-start | bytes 1572872 | tf_op jit(solution)/shard_map/ppermute | solution.py:29
  17.1 13.6 %copy-start.2 = (bf16[16,2048]{1,0:T(8,128)(2,1)S(1)}, bf16[16,2048]{1,0:T(8,128)(2,1)}, u32[]{:S(2)}) copy-start(bf16[16,2048]{1,0:T(8,128)(2,1)} %hidden.1) | copy-start | bytes 196612
  17.1 13.6 %copy-start.4 = (f32[2048]{0:T(1024)S(1)}, f32[2048]{0:T(1024)}, u32[]{:S(2)}) copy-start(f32[2048]{0:T(1024)} %param.25) | copy-start | bytes 24580
  17.1 17.7 %collective-permute-start.5 = (bf16[2,64,2048]{2,1,0:T(8,128)(2,1)S(1)}, bf16[2,64,2048]{2,1,0:T(8,128)(2,1)S(1)}, u32[]{:S(2)}, u32[]{:S(2)}) collective-permute-start(bf16[2,64,2048]{2,1,0:T(8,128)(2,1)S(1)} %get-tuple-element.19), channel_id=1, source_target_pairs={{0,6},{1,7},{2,4},{3,5},{4,10},{5,11},{6,8},{7,9},{8,14},{9,15},{1... | collective-permute-start | bytes 1572872 | tf_op jit(solution)/shard_map/ppermute | solution.py:302
  19.1 16.7 %collective-permute-start.2 = (bf16[2,64,2048]{2,1,0:T(8,128)(2,1)S(1)}, bf16[2,64,2048]{2,1,0:T(8,128)(2,1)S(1)}, u32[]{:S(2)}, u32[]{:S(2)}) collective-permute-start(bf16[2,64,2048]{2,1,0:T(8,128)(2,1)S(1)} %collective-permute-done.refs_0_), channel_id=1, source_target_pairs={{0,8},{1,9},{2,10},{3,11},{4,5},{5,4},{6,7},{7,6},{8,16},{9,17},{1... | collective-permute-start | bytes 1572872 | tf_op jit(solution)/shard_map/ppermute | solution.py:302
  20.5 19.8 %collective-permute-start.4 = (bf16[2,64,2048]{2,1,0:T(8,128)(2,1)S(1)}, bf16[2,64,2048]{2,1,0:T(8,128)(2,1)S(1)}, u32[]{:S(2)}, u32[]{:S(2)}) collective-permute-start(bf16[2,64,2048]{2,1,0:T(8,128)(2,1)S(1)} %collective-permute-done.3.refs_1_), channel_id=1, source_target_pairs={{1,9},{5,13},{9,17},{13,21},{17,25},{21,29},{25,1},{29,5}} | collective-permute-start | bytes 1572872 | tf_op jit(solution)/shard_map/ppermute | solution.py:302
  29.4 1.3 %collective-permute-start.1 = (bf16[16,2048]{1,0:T(8,128)(2,1)S(1)}, bf16[16,2048]{1,0:T(8,128)(2,1)S(1)}, u32[]{:S(2)}, u32[]{:S(2)}) collective-permute-start(bf16[16,2048]{1,0:T(8,128)(2,1)S(1)} %attention.3.refs_0_), channel_id=1, source_target_pairs={{0,1},{1,0},{2,3},{3,2},{4,5},{5,4},{6,7},{7,6},{8,9},{9,8},{10,11... | collective-permute-start | bytes 196616 | tf_op jit(solution)/shard_map/ppermute | solution.py:29
